TPU v7x, 128 devices: a whole 4x4x4 slice. The times are simulated.
128 devices in a mesh: pipe: 16 (over x, y_hi, core), dp: 8 (over z, y_lo).
Axes of the slice: x: 4, y: 4 (y_hi: 2, y_lo: 2; y = y_hi * 2 + y_lo), z: 4, core: 2. Of those that a mesh axis runs over, the one named last changes fastest.
Arguments:
- layer_input: bfloat16 [16, 2, 512, 3584], P('pipe', None, 'dp'), may hold values from -6 to 6
- residual_after: bfloat16 [16, 2, 512, 3584], P('pipe', None, 'dp'), may hold values from -6 to 6
- upstream: bfloat16 [16, 2, 512, 3584], P('pipe', None, 'dp'), may hold values from -6 to 6
- segment_lengths: int32 [16, 2, 4], P('pipe'), may hold values from 1 to 256, 512 in all within a row
- project_weight: bfloat16 [16, 3584, 8, 384], P('pipe', None, 'dp'), may hold values from -0.09375 to 0.09375
- output_weight: bfloat16 [16, 8, 128, 3584], P('pipe', 'dp'), may hold values from -0.1875 to 0.1875
- expand_weight: bfloat16 [16, 2, 2048, 3584], P('pipe', None, 'dp'), may hold values from -0.09375 to 0.09375
- reduce_weight: bfloat16 [16, 2048, 3584], P('pipe', 'dp'), may hold values from -0.125 to 0.125
Outputs:
- arriving: bfloat16 [16, 2, 512, 3584], P('pipe', None, 'dp')
- project_gradient: bfloat16 [16, 3584, 8, 384], P('pipe', None, 'dp')
- output_gradient: bfloat16 [16, 8, 128, 3584], P('pipe', 'dp')
- expand_gradient: bfloat16 [16, 2, 2048, 3584], P('pipe', None, 'dp')
- reduce_gradient: bfloat16 [16, 2048, 3584], P('pipe', 'dp')
Inputs may be any that keep to these rules, and one draw needn't show every extreme that they name: `segment_lengths`: the 4 lengths of one micro-batch sum to 512; the longest is 256.
All inputs are finite; a program needn't handle non-finite values.
Results may differ from a plain program's by a relative error of at most 0.023.
Values may be sent and summed in bfloat16 or wider, within the bound.
No kernel may reach another device: no remote copies, remote signals or barrier semaphores. Data moves between devices by JAX's collectives and lax.ppermute only.
A program may use at most 192 MiB of HBM per device.

v0:
```python
import jax
import jax.numpy as jnp
from jax import lax
from jax.sharding import PartitionSpec as P

EPSILON = 1e-06


def extended(value, sides, width):
    for axis, dim in sides:
        peers, length = (lax.axis_size(axis), value.shape[dim])
        up = [(i, (i + 1) % peers) for i in range(peers)]
        down = [(j, i) for i, j in up]
        last = lax.slice_in_dim(value, length - width, length, axis=dim)
        initial = lax.slice_in_dim(value, 0, width, axis=dim)
        before = lax.ppermute(last, axis, up)
        after = lax.ppermute(initial, axis, down)
        value = jnp.concatenate([before, value, after], axis=dim)
    return value


def rms_scale(values):
    return lax.rsqrt(jnp.mean(values * values, axis=-1, keepdims=True) + EPSILON)


def norm_back(values, row_scale, incoming):
    cubed = row_scale * row_scale * row_scale
    return row_scale * incoming - values * cubed * jnp.mean(
        incoming * values, axis=-1, keepdims=True
    )


def segment_mask(lengths, row_count):
    position = jnp.arange(row_count, dtype=jnp.int32)
    segment_ends = jnp.cumsum(lengths)
    segment_index = jnp.sum((position[:, None] >= segment_ends[None, :]).astype(jnp.int32), axis=1)
    same_doc = segment_index[:, None] == segment_index[None, :]
    return same_doc & (position[None, :] <= position[:, None])


def on_device(
    layer_input,
    residual_after,
    upstream,
    segment_lengths,
    project_weight,
    output_weight,
    expand_weight,
    reduce_weight,
):
    rows_own = layer_input.shape[2]
    group_size = lax.axis_size("dp")
    group_rank = lax.axis_index("dp")
    total_rows = rows_own * group_size
    first_row = group_rank * rows_own
    head_width = output_weight.shape[2]
    inputs_all, middle_all, incoming_all = (
        lax.all_gather(layer_input, "dp", axis=2, tiled=True),
        lax.all_gather(residual_after, "dp", axis=2, tiled=True),
        lax.all_gather(upstream, "dp", axis=2, tiled=True),
    )
    project_local = project_weight[0]
    output_local = output_weight[0]
    expand_local = expand_weight[0]
    reduce_local = reduce_weight[0]
    total_project = jnp.zeros(project_local.shape, jnp.float32)
    total_output = jnp.zeros(output_local.shape, jnp.float32)
    total_expand = jnp.zeros(expand_local.shape, jnp.float32)
    total_reduce = jnp.zeros(reduce_local.shape, jnp.float32)
    handed = []
    for batch_slot in range(2):
        layer_full = inputs_all[0, batch_slot].astype(jnp.float32)
        scale_layer = rms_scale(layer_full)
        layer_norm = (layer_full * scale_layer).astype(jnp.bfloat16)
        middle_full = middle_all[0, batch_slot].astype(jnp.float32)
        scale_middle = rms_scale(middle_full)
        middle_norm = (middle_full * scale_middle).astype(jnp.bfloat16)
        incoming = incoming_all[0, batch_slot]
        projected = jnp.einsum(
            "nd,dhe->nhe", layer_norm, project_local, preferred_element_type=jnp.float32
        ).astype(jnp.bfloat16)
        query_rows = projected[:, :, :head_width]
        key_rows = projected[:, :, head_width : 2 * head_width]
        value_rows = projected[:, :, 2 * head_width :]
        allowed = segment_mask(segment_lengths[0, batch_slot], total_rows)
        scores = jnp.einsum(
            "nhe,mhe->hnm", query_rows, key_rows, preferred_element_type=jnp.float32
        ) * head_width ** (-0.5)
        weights = jnp.where(allowed[None], jnp.exp(scores), 0.0)
        softmax_rows = weights / jnp.sum(weights, axis=-1, keepdims=True)
        softmax_low = softmax_rows.astype(jnp.bfloat16)
        attended = jnp.einsum(
            "hnm,mhe->nhe", softmax_low, value_rows, preferred_element_type=jnp.float32
        ).astype(jnp.bfloat16)
        pair_pre = jnp.einsum(
            "nd,kfd->knf", middle_norm, expand_local, preferred_element_type=jnp.float32
        )
        gate_pre = pair_pre[0]
        up_pre = pair_pre[1]
        gate_sigmoid = jax.nn.sigmoid(gate_pre)
        hidden = (gate_pre * gate_sigmoid * up_pre).astype(jnp.bfloat16)
        back_hidden = jnp.einsum(
            "nd,fd->nf", incoming, reduce_local, preferred_element_type=jnp.float32
        )
        back_gate = back_hidden * up_pre * gate_sigmoid * (1.0 + gate_pre * (1.0 - gate_sigmoid))
        back_up = back_hidden * gate_pre * gate_sigmoid
        back_pair = jnp.stack([back_gate, back_up]).astype(jnp.bfloat16)
        total_reduce = total_reduce + jnp.einsum(
            "nf,nd->fd", hidden, incoming, preferred_element_type=jnp.float32
        )
        total_expand = total_expand + jnp.einsum(
            "knf,nd->kfd", back_pair, middle_norm, preferred_element_type=jnp.float32
        )
        branch_full = jnp.einsum(
            "knf,kfd->nd", back_pair, expand_local, preferred_element_type=jnp.float32
        )
        back_middle_norm = lax.psum(branch_full.astype(jnp.bfloat16), "dp").astype(jnp.float32)
        back_middle = incoming.astype(jnp.float32) + norm_back(
            middle_full, scale_middle, back_middle_norm
        )
        back_middle_low = back_middle.astype(jnp.bfloat16)
        back_middle_own = lax.dynamic_slice_in_dim(back_middle, first_row, rows_own, 0)
        back_attended = jnp.einsum(
            "nd,hed->nhe", back_middle_low, output_local, preferred_element_type=jnp.float32
        ).astype(jnp.bfloat16)
        total_output = total_output + jnp.einsum(
            "nhe,nd->hed", attended, back_middle_low, preferred_element_type=jnp.float32
        )
        back_softmax = jnp.einsum(
            "nhe,mhe->hnm", back_attended, value_rows, preferred_element_type=jnp.float32
        )
        centre = jnp.sum(softmax_rows * back_softmax, axis=-1, keepdims=True)
        back_scores = (softmax_rows * (back_softmax - centre) * head_width ** (-0.5)).astype(
            jnp.bfloat16
        )
        back_query = jnp.einsum(
            "hnm,mhe->nhe", back_scores, key_rows, preferred_element_type=jnp.float32
        )
        back_key = jnp.einsum(
            "hnm,nhe->mhe", back_scores, query_rows, preferred_element_type=jnp.float32
        )
        back_value = jnp.einsum(
            "hnm,nhe->mhe", softmax_low, back_attended, preferred_element_type=jnp.float32
        )
        back_project = jnp.concatenate([back_query, back_key, back_value], axis=-1).astype(
            jnp.bfloat16
        )
        total_project = total_project + jnp.einsum(
            "nd,nhe->dhe", layer_norm, back_project, preferred_element_type=jnp.float32
        )
        back_layer_own = lax.psum_scatter(
            jnp.einsum(
                "nhe,dhe->nd", back_project, project_local, preferred_element_type=jnp.float32
            ).astype(jnp.bfloat16),
            "dp",
            scatter_dimension=0,
            tiled=True,
        ).astype(jnp.float32)
        layer_own = layer_input[0, batch_slot].astype(jnp.float32)
        scale_layer_own = lax.dynamic_slice_in_dim(scale_layer, first_row, rows_own, 0)
        back_input = (
            back_middle_own + norm_back(layer_own, scale_layer_own, back_layer_own)
        ).astype(jnp.bfloat16)
        handed.append(back_input)
    wrapped_pair = extended(jnp.stack(handed), (("pipe", 0),), 1)
    passing = [wrapped_pair[3], wrapped_pair[0]]
    arriving = jnp.stack(passing)[None]
    return (
        arriving,
        total_project.astype(jnp.bfloat16)[None],
        total_output.astype(jnp.bfloat16)[None],
        total_expand.astype(jnp.bfloat16)[None],
        total_reduce.astype(jnp.bfloat16)[None],
    )


def solution(mesh):
    return jax.shard_map(
        on_device,
        mesh=mesh,
        in_specs=(
            P("pipe", None, "dp", None),
            P("pipe", None, "dp", None),
            P("pipe", None, "dp", None),
            P("pipe", None, None),
            P("pipe", None, "dp", None),
            P("pipe", "dp", None, None),
            P("pipe", None, "dp", None),
            P("pipe", "dp", None),
        ),
        out_specs=(
            P("pipe", None, "dp", None),
            P("pipe", None, "dp", None),
            P("pipe", "dp", None, None),
            P("pipe", None, "dp", None),
            P("pipe", "dp", None),
        ),
        check_vma=False,
    )
```

profile of v0, /device:TPU:1, one launch (start us, length us, event | category | flops | bytes accessed | tf_op | source)
XLA Modules:
  0.0 990.8 jit_solution(17538528393815608258)
XLA Ops:
  7.2 0.7 all-gather.6.cloned.1.call-update
  8.0 0.7 all-gather.4.cloned.1.call-update
  8.7 0.7 all-gather.8.cloned.1.call-update
  9.4 152.1 %all-gather.6.cloned.1.call-done = bf16[1,2,512,3584]{3,2,1,0:T(8,128)(2,1)} async-done(((bf16[1,2,64,3584]{3,2,1,0:T(8,128)(2,1)}), bf16[1,2,512,3584]{3,2,1,0:T(8,128)(2,1)}) %all-gather.6.cloned.1.call-update) | async-done | bytes 7340048 | tf_op jit(solution)/shard_map/all_gather | solution.py:59
  161.6 4.1 fusion.16
  165.7 1.1 copy-done.1
  166.8 5.1 fusion.95
  171.9 141.1 %all-gather.4.cloned.1.call-done = bf16[1,2,512,3584]{3,2,1,0:T(8,128)(2,1)} async-done(((bf16[1,2,64,3584]{3,2,1,0:T(8,128)(2,1)}), bf16[1,2,512,3584]{3,2,1,0:T(8,128)(2,1)}) %all-gather.4.cloned.1.call-update) | async-done | bytes 7340048 | tf_op jit(solution)/shard_map/all_gather | solution.py:60
  313.0 4.2 fusion.187
  317.2 3.9 bitcast_convert_fusion.1
  321.1 4.3 fusion.100
  325.5 1.2 fusion.188
  326.7 0.7 copy-done.11
  327.4 3.9 bitcast_convert_fusion
  332.8 131.7 %all-gather.8.cloned.1.call-done = bf16[1,2,512,3584]{3,2,1,0:T(8,128)(2,1)} async-done(((bf16[1,2,64,3584]{3,2,1,0:T(8,128)(2,1)}), bf16[1,2,512,3584]{3,2,1,0:T(8,128)(2,1)}) %all-gather.8.cloned.1.call-update) | async-done | bytes 7340048 | tf_op jit(solution)/shard_map/all_gather | solution.py:58
  464.4 4.1 fusion.21
  468.6 1.1 copy-done.5
  469.7 2.1 fusion.119
  471.8 1.3 fusion.204
  473.2 296.1 %all-reduce.3.cloned.1.call-done = (bf16[512,3584]{1,0:T(8,128)(2,1)}, bf16[512,3584]{1,0:T(8,128)(2,1)}) async-done(((bf16[512,3584]{1,0:T(8,128)(2,1)}, bf16[512,3584]{1,0:T(8,128)(2,1)}), (bf16[512,3584]{1,0:T(8,128)(2,1)}, bf16[512,3584]{1,0:T(8,128)(2,1)})) %all-reduce.3.cloned.1.call-update) | async-done | bytes 7340048 | tf_op jit(solution)/shard_map/psum | solution.py:117
  769.3 6.4 fusion.18
  775.7 1.0 copy-done.4
  776.7 10.9 %fusion.13 = (f32[512,3584]{1,0:T(8,128)}, f32[512,3584]{1,0:T(8,128)S(1)}) fusion(bf16[512,3584]{1,0:T(8,128)(2,1)S(1)} %copy-done.4, f32[512]{0:T(512)S(1)} %broadcast_multiply_fusion.1, f32[512]{0:T(512)S(1)} %get-tuple-element.42, f32[512]{0:T(512)S(1)} %get-tuple-element.41, bf16[1,2,512,3584]{3,2,1,0:T(8,128)(2,1)} %all-gather.4.cloned.1.call-done, ...), kind=kLoop, calls=%fused_computation.23 | loop fusion | flops 29360128 | bytes 36712448 | tf_op jit(solution)/shard_map/add | solution.py:118
  787.6 1.1 fusion.132
  788.7 1.8 copy-done.2
  792.3 3.9 convolution_convert_fusion
  796.8 4.3 fusion.124
  801.5 1.1 fusion.129
  805.1 4.0 convolution_convert_fusion.1
  809.2 1.4 fusion.191
  810.6 1.3 fusion.192
  811.8 3.7 fusion.71
  815.6 4.5 fusion.57
  820.1 4.6 fusion.36
  824.8 4.4 fusion.33
  829.2 5.1 fusion.51
  834.3 5.6 fusion.91
  839.9 7.7 fusion.35
  847.6 31.5 %reduce-scatter.5.cloned.1.call-done = bf16[64,3584]{1,0:T(8,128)(2,1)} async-done(((bf16[512,3584]{1,0:T(8,128)(2,1)}), bf16[64,3584]{1,0:T(8,128)(2,1)}) %reduce-scatter.5.cloned.1.call-update) | async-done | bytes 458768 | tf_op jit(solution)/shard_map/reduce_scatter | solution.py:151
  879.1 83.7 %reduce-scatter.3.cloned.1.call-done = bf16[64,3584]{1,0:T(8,128)(2,1)} async-done(((bf16[512,3584]{1,0:T(8,128)(2,1)}), bf16[64,3584]{1,0:T(8,128)(2,1)}) %reduce-scatter.3.cloned.1.call-update) | async-done | bytes 458768 | tf_op jit(solution)/shard_map/reduce_scatter | solution.py:151
  962.8 1.8 fusion.152
  964.6 3.4 fusion.176
  968.0 0.8 collective-permute-start
  968.8 2.4 collective-permute-start.1
  971.2 5.7 fusion.38
  977.0 0.7 collective-permute-done
  977.7 3.9 collective-permute-done.1
  981.6 2.2 maximum_bitcast_fusion
  (126 shorter events, 6.9 us)
Async XLA Ops:
  7.2 461.4 %copy-start = (bf16[1,3584,1,384]{3,1,2,0:T(8,128)(2,1)S(1)}, bf16[1,3584,1,384]{3,1,2,0:T(8,128)(2,1)}, u32[]{:S(2)}) copy-start(bf16[1,3584,1,384]{3,1,2,0:T(8,128)(2,1)} %param.12) | copy-start | bytes 8257540
  7.2 154.4 %all-gather.6.cloned.1.call-start = ((), (), s32[]{:S(2)}) async-start(), calls=%async_computation.3 | async-start | bytes 8257536 | tf_op jit(solution)/shard_map/all_gather | solution.py:59
  7.9 305.1 %all-gather.4.cloned.1.call-start = ((), (), s32[]{:S(2)}) async-start(), calls=%async_computation.2 | async-start | bytes 8257536 | tf_op jit(solution)/shard_map/all_gather | solution.py:60
  8.7 455.8 %all-gather.8.cloned.1.call-start = ((), (), s32[]{:S(2)}) async-start(), calls=%async_computation.4 | async-start | bytes 8257536 | tf_op jit(solution)/shard_map/all_gather | solution.py:58
  9.4 759.9 %all-reduce.3.cloned.1.call-start = ((), (), s32[]{:S(2)}) async-start(), calls=%async_computation.7 | async-start | bytes 14680064 | tf_op jit(solution)/shard_map/psum | solution.py:117
  161.6 5.2 copy-start.1
  313.0 4.2 copy-start.35
  317.2 3.9 copy-start.15
  317.2 3.9 copy-start.17
  317.2 8.2 slice-start.4
  321.1 4.3 slice-start.5
  321.1 4.3 copy-start.36
  331.3 547.7 %reduce-scatter.5.cloned.1.call-start = ((), (), s32[]{:S(2)}) async-start(), calls=%async_computation.6 | async-start | bytes 4128768 | tf_op jit(solution)/shard_map/reduce_scatter | solution.py:151
  464.4 5.3 copy-start.5
  468.5 3.3 copy-start.25
  468.5 328.2 %copy-start.27 = (f32[512]{0:T(512)}, f32[512]{0:T(512)S(1)}, u32[]{:S(2)}) copy-start(f32[512]{0:T(512)S(1)} %get-tuple-element.44) | copy-start | bytes 6148
  471.8 319.5 %copy-start.10 = (bf16[512,1,384]{2,0,1:T(8,128)(2,1)}, bf16[512,1,384]{2,0,1:T(8,128)(2,1)S(1)}, u32[]{:S(2)}) copy-start(bf16[512,1,384]{2,0,1:T(8,128)(2,1)S(1)} %fusion.119) | copy-start | bytes 1179652
  769.3 6.4 copy-start.3
  769.3 7.4 copy-start.4
  776.7 10.9 %copy-start.8 = (bf16[1,1,128,3584]{3,2,1,0:T(8,128)(2,1)S(1)}, bf16[1,1,128,3584]{3,2,1,0:T(8,128)(2,1)}, u32[]{:S(2)}) copy-start(bf16[1,1,128,3584]{3,2,1,0:T(8,128)(2,1)} %param.13) | copy-start | bytes 2752516
  787.6 2.9 copy-start.2
  787.6 2.9 copy-start.6
  792.3 4.4 copy-start.37
  792.3 4.2 copy-start.34
  796.3 166.5 %reduce-scatter.3.cloned.1.call-start = ((), (), s32[]{:S(2)}) async-start(), calls=%async_computation.5 | async-start | bytes 4128768 | tf_op jit(solution)/shard_map/reduce_scatter | solution.py:151
  796.8 4.7 slice-start.2
  796.8 4.7 slice-start.3
  796.8 4.7 copy-start.9
  809.2 6.4 copy-start.16
  809.2 6.4 copy-start.18
  811.8 12.9 %slice-start = ((s8[7340032]{0:T(1024)(128)(4,1)}), s8[4194304]{0:T(1024)(128)(4,1)S(1)}, s32[]{:S(2)}) async-start(s8[7340032]{0:T(1024)(128)(4,1)} %bitcast.394), calls=%async_computation.8 | async-start | bytes 8388608
  815.6 4.5 copy-start.14
  815.6 9.1 slice-start.1
  820.1 4.7 copy-start.12
  820.1 9.1 slice-start.6
  824.7 4.5 slice-start.7
  824.7 4.5 copy-start.22
  824.8 4.4 copy-start.24
  824.8 4.4 copy-start.28
  824.8 4.4 copy-start.39
  834.3 5.6 copy-start.20
  834.3 5.6 copy-start.26
  839.9 124.7 %copy-start.29 = (f32[64]{0:T(128)S(1)}, f32[64]{0:T(128)}, u32[]{:S(2)}) copy-start(f32[64]{0:T(128)} %get-tuple-element.15) | copy-start | bytes 772
  839.9 124.7 %copy-start.30 = (f32[64]{0:T(128)S(1)}, f32[64]{0:T(128)}, u32[]{:S(2)}) copy-start(f32[64]{0:T(128)} %get-tuple-element.16) | copy-start | bytes 772
  839.9 124.7 %copy-start.31 = (f32[64]{0:T(128)S(1)}, f32[64]{0:T(128)}, u32[]{:S(2)}) copy-start(f32[64]{0:T(128)} %get-tuple-element.17) | copy-start | bytes 772
  839.9 124.7 %copy-start.32 = (f32[64]{0:T(128)S(1)}, f32[64]{0:T(128)}, u32[]{:S(2)}) copy-start(f32[64]{0:T(128)} %get-tuple-element.18) | copy-start | bytes 772
  968.0 9.7 collective-permute-start
  968.8 12.8 %collective-permute-start.1 = (bf16[1,64,3584]{2,1,0:T(8,128)(2,1)S(1)}, bf16[1,64,3584]{2,1,0:T(8,128)(2,1)}, u32[]{:S(2)}, u32[]{:S(2)}) collective-permute-start(bf16[1,64,3584]{2,1,0:T(8,128)(2,1)S(1)} %get-tuple-element.26), channel_id=1, source_target_pairs={{0,8},{8,16},{16,24},{24,32},{32,40},{40,48},{48,56},{56,64},{64,7... | collective-permute-start | bytes 1376264 | tf_op jit(solution)/shard_map/ppermute | solution.py:16
  (8 other events, 7.6 us)
Sparse Core Ops, SparseCore 0:
  9.7 151.8 all-gather.5
  163.2 149.7 all-gather.3
  314.6 149.7 all-gather.7
  467.4 301.8 all-reduce.2
  796.4 82.6 reduce-scatter.4
  881.4 81.3 reduce-scatter.2
where the time goes:
time: 999 us; the launch traced here: 991 us
  waiting for transfers between devices  843 us (84%)
  matrix products  84.4 us (8%)
  other arithmetic  36.5 us (4%)
  between operations  15 us (2%)
    psum x1, waiting for transfers between devices, on_device(): lax.psum(branch_full.astype(jnp.bfloat16), 'dp').astype(jnp.float32)  296 us
    all_gather x1, waiting for transfers between devices, on_device(): lax.all_gather(residual_after, 'dp', axis=2, tiled=True)  152 us
    all_gather x1, waiting for transfers between devices, on_device(): lax.all_gather(upstream, 'dp', axis=2, tiled=True)  141 us
    all_gather x1, waiting for transfers between devices, on_device(): lax.all_gather(layer_input, 'dp', axis=2, tiled=True)  132 us
    reduce_scatter x2, waiting for transfers between devices, on_device(): lax.psum_scatter(jnp.einsum('nhe,dhe->nd', back_project, project_local, p...  115 us
  transfers between devices with their start and end apart: 8, of which 8 were waited for; matrix products, arithmetic and copies ran while one was open for 9% of the time, Pallas kernels for 0%

commit v1 on v0

v1 whole, which is shorter than its diff:
```python
import jax
import jax.numpy as jnp
from jax import lax
from jax.sharding import PartitionSpec as P

EPSILON = 1e-06


def rms_scale(values):
    return lax.rsqrt(jnp.mean(values * values, axis=-1, keepdims=True) + EPSILON)


def norm_back(values, row_scale, incoming):
    cubed = row_scale * row_scale * row_scale
    return row_scale * incoming - values * cubed * jnp.mean(
        incoming * values, axis=-1, keepdims=True
    )


def shift(value, dz, dy):
    pairs = [(i, ((i // 2 + dz) % 4) * 2 + ((i % 2) ^ dy)) for i in range(8)]
    return lax.ppermute(value, "dp", pairs)


def gather_blocks(own):
    over = shift(own, 0, 1)
    below = shift(own, 1, 0)
    above = shift(own, -1, 0)
    below_over = shift(over, 1, 0)
    above_over = shift(over, -1, 0)
    far = shift(below, 1, 0)
    far_over = shift(above_over, -1, 0)
    return [[own, over], [above, above_over], [far, far_over], [below, below_over]]


def scatter_sum(parts):
    wide = lambda value: value.astype(jnp.float32)
    low = lambda value: value.astype(jnp.bfloat16)
    from_below = shift(parts[2][0], 1, 0)
    from_above = shift(parts[2][1], -1, 0)
    up_own = shift(low(wide(parts[1][0]) + wide(from_below)), 1, 0)
    up_over = shift(parts[1][1], 1, 0)
    down_own = shift(parts[3][0], -1, 0)
    down_over = shift(low(wide(parts[3][1]) + wide(from_above)), -1, 0)
    over = shift(low(wide(parts[0][1]) + wide(up_over) + wide(down_over)), 0, 1)
    return wide(parts[0][0]) + wide(up_own) + wide(down_own) + wide(over)


def blocks_of(rows):
    return [[rows[(2 * dz + dy) * 64 : (2 * dz + dy + 1) * 64] for dy in range(2)] for dz in range(4)]


def joined(blocks):
    return jnp.concatenate([blocks[dz][dy] for dz in range(4) for dy in range(2)], axis=-2)


def segment_mask(lengths, position):
    segment_ends = jnp.cumsum(lengths)
    segment_index = jnp.sum((position[:, None] >= segment_ends[None, :]).astype(jnp.int32), axis=1)
    same_doc = segment_index[:, None] == segment_index[None, :]
    return same_doc & (position[None, :] <= position[:, None])


def dot(spec, left, right):
    return jnp.einsum(spec, left, right, preferred_element_type=jnp.float32)


def on_device(
    layer_input,
    residual_after,
    upstream,
    segment_lengths,
    project_weight,
    output_weight,
    expand_weight,
    reduce_weight,
):
    rank = lax.axis_index("dp")
    z, y = rank // 2, rank % 2
    position = jnp.concatenate(
        [
            (((z + dz) % 4) * 2 + (y ^ dy)) * 64 + jnp.arange(64, dtype=jnp.int32)
            for dz in range(4)
            for dy in range(2)
        ]
    )
    project = project_weight[0, :, 0]
    output = output_weight[0, 0]
    expand = expand_weight[0].reshape(512, 3584)
    reduce = reduce_weight[0]
    pairs = [
        gather_blocks(jnp.stack([residual_after[0, slot], upstream[0, slot]])) for slot in range(2)
    ]
    layers = gather_blocks(layer_input[0])
    layers = joined(layers)
    norms, hiddens, backs, comings, leaves = [], [], [], [], []
    for slot in range(2):
        both = joined(pairs[slot])
        middle_full = both[0].astype(jnp.float32)
        incoming = both[1]
        middle_norm = (middle_full * rms_scale(middle_full)).astype(jnp.bfloat16)
        pre = dot("nd,fd->nf", middle_norm, expand)
        gate_pre, up_pre = pre[:, :256], pre[:, 256:]
        back_hidden = dot("nd,fd->nf", incoming, reduce)
        gate_sigmoid = jax.nn.sigmoid(gate_pre)
        silu = gate_pre * gate_sigmoid
        hidden = (silu * up_pre).astype(jnp.bfloat16)
        back_gate = back_hidden * up_pre * gate_sigmoid * (1.0 + gate_pre * (1.0 - gate_sigmoid))
        back_up = back_hidden * silu
        back_pair = jnp.concatenate([back_gate, back_up], axis=1).astype(jnp.bfloat16)
        branch = dot("nf,fd->nd", back_pair, expand).astype(jnp.bfloat16)
        norms.append(middle_norm)
        hiddens.append(hidden)
        backs.append(back_pair)
        comings.append(incoming)
        own_norm_back = scatter_sum(blocks_of(branch))
        own_middle = residual_after[0, slot].astype(jnp.float32)
        back_middle = upstream[0, slot].astype(jnp.float32) + norm_back(
            own_middle, rms_scale(own_middle), own_norm_back
        )
        leaves.append(back_middle)
    layer_norms, attends, lows, projects, handed = [], [], [], [], []
    for slot in range(2):
        back_middle = leaves[slot]
        back_middle_low = joined(gather_blocks(back_middle.astype(jnp.bfloat16)))
        layer_full = layers[slot].astype(jnp.float32)
        layer_norm = (layer_full * rms_scale(layer_full)).astype(jnp.bfloat16)
        projected = dot("nd,de->ne", layer_norm, project).astype(jnp.bfloat16)
        query, key, value = projected[:, :128], projected[:, 128:256], projected[:, 256:]
        allowed = segment_mask(segment_lengths[0, slot], position)
        scores = dot("ne,me->nm", query, key) * 128 ** (-0.5)
        weights = jnp.where(allowed, jnp.exp(scores), 0.0)
        softmax_rows = weights / jnp.sum(weights, axis=-1, keepdims=True)
        softmax_low = softmax_rows.astype(jnp.bfloat16)
        attended = dot("nm,me->ne", softmax_low, value).astype(jnp.bfloat16)
        back_attended = dot("nd,ed->ne", back_middle_low, output).astype(jnp.bfloat16)
        back_softmax = dot("ne,me->nm", back_attended, value)
        centre = jnp.sum(softmax_rows * back_softmax, axis=-1, keepdims=True)
        back_scores = (softmax_rows * (back_softmax - centre) * 128 ** (-0.5)).astype(jnp.bfloat16)
        back_query = dot("nm,me->ne", back_scores, key)
        back_key = dot("nm,ne->me", back_scores, query)
        back_value = dot("nm,ne->me", softmax_low, back_attended)
        back_project = jnp.concatenate([back_query, back_key, back_value], axis=-1).astype(
            jnp.bfloat16
        )
        terms = dot("ne,de->nd", back_project, project).astype(jnp.bfloat16)
        own_layer_back = scatter_sum(blocks_of(terms))
        own_layer = layer_input[0, slot].astype(jnp.float32)
        back_input = back_middle + norm_back(own_layer, rms_scale(own_layer), own_layer_back)
        step = -1 if slot == 0 else 1
        handed.append(
            lax.ppermute(
                back_input.astype(jnp.bfloat16), "pipe", [(i, (i + step) % 16) for i in range(16)]
            )
        )
        layer_norms.append(layer_norm)
        attends.append(attended)
        lows.append(back_middle_low)
        projects.append(back_project)

    def total(lefts, rights):
        left = jnp.concatenate(lefts, axis=0)
        right = jnp.concatenate(rights, axis=0)
        return dot("na,nb->ab", left, right).astype(jnp.bfloat16)

    return (
        jnp.stack(handed)[None],
        total(layer_norms, projects)[None, :, None],
        total(attends, lows)[None, None],
        total(backs, norms).reshape(1, 2, 256, 3584),
        total(hiddens, comings)[None],
    )


def solution(mesh):
    return jax.shard_map(
        on_device,
        mesh=mesh,
        in_specs=(
            P("pipe", None, "dp", None),
            P("pipe", None, "dp", None),
            P("pipe", None, "dp", None),
            P("pipe", None, None),
            P("pipe", None, "dp", None),
            P("pipe", "dp", None, None),
            P("pipe", None, "dp", None),
            P("pipe", "dp", None),
        ),
        out_specs=(
            P("pipe", None, "dp", None),
            P("pipe", None, "dp", None),
            P("pipe", "dp", None, None),
            P("pipe", None, "dp", None),
            P("pipe", "dp", None),
        ),
        check_vma=False,
    )
```

time: 999 us -> 503 us (0.50)
  waiting for transfers between devices: 843 us -> 293 us
  starting transfers between devices: 4.12 us -> 86.2 us
  matrix products: 84.4 us -> 54.8 us
  local copies, waits for them, and re-layouts: 7.8 us -> 25 us
  between operations: 15 us -> 1.74 us
    all_gather x3 -> x0, waiting for transfers between devices: 425 us -> none  [the longest x1 152 us: on_device(): lax.all_gather(residual_after, 'dp', axis=2, tiled=True)]
    psum x1 -> x0, waiting for transfers between devices: 296 us -> none  [on_device(): lax.psum(branch_full.astype(jnp.bfloat16), 'dp').astype(jnp.float32)]
    ppermute x2 -> x65, waiting for transfers between devices: 4.6 us -> 293 us  [the longest x63 284 us: shift(): return lax.ppermute(value, 'dp', pairs)]
    reduce_scatter x2 -> x0, waiting for transfers between devices: 115 us -> none  [on_device(): lax.psum_scatter(jnp.einsum('nhe,dhe->nd', back_project, project_local, p...]
    ppermute x2 -> x65, starting transfers between devices: 3.25 us -> 86.2 us  [the longest x63 71.5 us: shift(): return lax.ppermute(value, 'dp', pairs)]
    dot_general x30 -> x28, matrix products: 84.4 us -> 54.8 us  [dot(): return jnp.einsum(spec, left, right, preferred_element_type=jnp.float32)]
    convert_element_type x2 -> x14, other arithmetic: 0.57 us -> 21.5 us  [the longest x8 6.84 us: scatter_sum(): low = lambda value: value.astype(jnp.bfloat16)]
    unnamed x96 -> x111, local copies, waits for them, and re-layouts: 7.29 us -> 18.5 us
  transfers between devices with their start and end apart: 8 -> 65, of which waited for: 8 -> 29; matrix products, arithmetic and copies ran while one was open for 9% -> 18% of each run, Pallas kernels for 0% -> 0%
where the time goes in v1:
time: 503 us; the launch traced here: 496 us
  waiting for transfers between devices  293 us (58%)
  starting transfers between devices  86.2 us (17%)
  matrix products  54.8 us (11%)
  other arithmetic  35 us (7%)
  local copies, waits for them, and re-layouts  25 us (5%)
    ppermute x63, waiting for transfers between devices, shift(): return lax.ppermute(value, 'dp', pairs)  284 us
    ppermute x63, starting transfers between devices, shift(): return lax.ppermute(value, 'dp', pairs)  71.5 us
    dot_general x28, matrix products, dot(): return jnp.einsum(spec, left, right, preferred_element_type=jnp.float32)  54.8 us
    unnamed x111, local copies, waits for them, and re-layouts  18.5 us
    ppermute x2, starting transfers between devices, on_device(): lax.ppermute(back_input.astype(jnp.bfloat16), 'pipe', [(i, (i + step) % 1...  14.8 us
  transfers between devices with their start and end apart: 65, of which 29 were waited for; matrix products, arithmetic and copies ran while one was open for 18% of the time, Pallas kernels for 0%

profile of v1, /device:TPU:1, one launch (start us, length us, event | category | flops | bytes accessed | tf_op | source)
XLA Modules:
  0.0 496.1 jit_solution(13876320191326928542)
XLA Ops:
  15.9 10.8 %collective-permute-done.14 = bf16[2,64,3584]{2,1,0:T(8,128)(2,1)} collective-permute-done((bf16[2,64,3584]{2,1,0:T(8,128)(2,1)}, bf16[2,64,3584]{2,1,0:T(8,128)(2,1)}, u32[]{:S(2)}, u32[]{:S(2)}) %collective-permute-start.14) | collective-permute-done | bytes 917536 | tf_op jit(solution)/shard_map/ppermute | solution.py:22
  33.7 12.6 %collective-permute-done.36 = bf16[2,64,3584]{2,1,0:T(8,128)(2,1)} collective-permute-done((bf16[2,64,3584]{2,1,0:T(8,128)(2,1)}, bf16[2,64,3584]{2,1,0:T(8,128)(2,1)}, u32[]{:S(2)}, u32[]{:S(2)}) %collective-permute-start.36) | collective-permute-done | bytes 917536 | tf_op jit(solution)/shard_map/ppermute | solution.py:22
  51.9 14.3 %collective-permute-done = bf16[2,64,3584]{2,1,0:T(8,128)(2,1)S(1)} collective-permute-done((bf16[2,64,3584]{2,1,0:T(8,128)(2,1)S(1)}, bf16[2,64,3584]{2,1,0:T(8,128)(2,1)S(1)}, u32[]{:S(2)}, u32[]{:S(2)}) %collective-permute-start) | collective-permute-done | bytes 917536 | tf_op jit(solution)/shard_map/ppermute | solution.py:22
  68.0 17.5 %collective-permute-done.16 = bf16[2,64,3584]{2,1,0:T(8,128)(2,1)S(1)} collective-permute-done((bf16[2,64,3584]{2,1,0:T(8,128)(2,1)}, bf16[2,64,3584]{2,1,0:T(8,128)(2,1)S(1)}, u32[]{:S(2)}, u32[]{:S(2)}) %collective-permute-start.16) | collective-permute-done | bytes 917536 | tf_op jit(solution)/shard_map/ppermute | solution.py:22
  87.4 23.3 %collective-permute-done.18 = bf16[2,64,3584]{2,1,0:T(8,128)(2,1)S(1)} collective-permute-done((bf16[2,64,3584]{2,1,0:T(8,128)(2,1)}, bf16[2,64,3584]{2,1,0:T(8,128)(2,1)S(1)}, u32[]{:S(2)}, u32[]{:S(2)}) %collective-permute-start.18) | collective-permute-done | bytes 917536 | tf_op jit(solution)/shard_map/ppermute | solution.py:22
  110.8 2.7 collective-permute-start.2
  114.5 35.5 %collective-permute-done.40 = bf16[2,64,3584]{2,1,0:T(8,128)(2,1)S(1)} collective-permute-done((bf16[2,64,3584]{2,1,0:T(8,128)(2,1)S(1)}, bf16[2,64,3584]{2,1,0:T(8,128)(2,1)S(1)}, u32[]{:S(2)}, u32[]{:S(2)}) %collective-permute-start.40) | collective-permute-done | bytes 917536 | tf_op jit(solution)/shard_map/ppermute | solution.py:22
  153.8 35.6 %collective-permute-done.4 = bf16[2,64,3584]{2,1,0:T(8,128)(2,1)S(1)} collective-permute-done((bf16[2,64,3584]{2,1,0:T(8,128)(2,1)S(1)}, bf16[2,64,3584]{2,1,0:T(8,128)(2,1)S(1)}, u32[]{:S(2)}, u32[]{:S(2)}) %collective-permute-start.4) | collective-permute-done | bytes 917536 | tf_op jit(solution)/shard_map/ppermute | solution.py:22
  192.9 2.9 fusion.85
  195.7 2.9 fusion.80
  198.6 10.2 %collective-permute-done.41 = bf16[2,64,3584]{2,1,0:T(8,128)(2,1)S(1)} collective-permute-done((bf16[2,64,3584]{2,1,0:T(8,128)(2,1)S(1)}, bf16[2,64,3584]{2,1,0:T(8,128)(2,1)S(1)}, u32[]{:S(2)}, u32[]{:S(2)}) %collective-permute-start.41) | collective-permute-done | bytes 917536 | tf_op jit(solution)/shard_map/ppermute | solution.py:22
  209.0 5.2 %fusion.12 = (bf16[512,3584]{1,0:T(8,128)(2,1)}, bf16[512,3584]{1,0:T(8,128)(2,1)}) fusion(f32[512]{0:T(512)S(1)} %get-tuple-element.114, bf16[2,512,3584]{2,1,0:T(8,128)(2,1)S(1)} %constant_dynamic-update-slice_fusion.8, f32[512]{0:T(512)S(1)} %get-tuple-element.113), kind=kLoop, calls=%fused_computation.20 | loop fusion | flops 11010048 | bytes 14684160 | tf_op jit(solution)/shard_map/convert_element_type | solution.py:127
  215.1 3.2 fusion.52
  218.3 2.9 fusion.15
  221.2 7.3 %collective-permute-done.5 = bf16[2,64,3584]{2,1,0:T(8,128)(2,1)S(1)} collective-permute-done((bf16[2,64,3584]{2,1,0:T(8,128)(2,1)S(1)}, bf16[2,64,3584]{2,1,0:T(8,128)(2,1)S(1)}, u32[]{:S(2)}, u32[]{:S(2)}) %collective-permute-start.5) | collective-permute-done | bytes 917536 | tf_op jit(solution)/shard_map/ppermute | solution.py:22
  232.0 2.9 fusion.9
  241.3 2.7 collective-permute-start.47
  243.9 2.8 collective-permute-start.45
  254.7 8.5 %fusion.32 = bf16[512,3584]{1,0:T(8,128)(2,1)} fusion(bf16[512,3584]{1,0:T(8,128)(2,1)S(1)} %copy-done.5, bf16[512,3584]{1,0:T(8,128)(2,1)} %fusion.9, bf16[512,256]{0,1:T(8,128)(2,1)} %copy-done.16, bf16[512,256]{0,1:T(8,128)(2,1)} %copy-done.15, bf16[512,256]{0,1:T(8,128)(2,1)} %copy-done.18, bf16[512,256]{0,1:T(8,128)(2,1)} %copy-done.17), kind=kOutput, calls=%fused_computation.44 | convolution fusion | flops 3778805760 | bytes 12058624 | tf_op jit(solution)/shard_map/na,nb->ab/dot_general | solution.py:65
  267.6 2.7 collective-permute-start.11
  271.6 2.7 collective-permute-start.9
  275.7 3.1 collective-permute-start.48
  280.1 14.9 %collective-permute-done.48 = bf16[64,3584]{1,0:T(8,128)(2,1)S(1)} collective-permute-done((bf16[64,3584]{1,0:T(8,128)(2,1)S(1)}, bf16[64,3584]{1,0:T(8,128)(2,1)S(1)}, u32[]{:S(2)}, u32[]{:S(2)}) %collective-permute-start.48) | collective-permute-done | bytes 458784 | tf_op jit(solution)/shard_map/ppermute | solution.py:22
  295.0 3.4 collective-permute-start.12
  298.7 6.5 %collective-permute-done.12 = bf16[64,3584]{1,0:T(8,128)(2,1)S(1)} collective-permute-done((bf16[64,3584]{1,0:T(8,128)(2,1)S(1)}, bf16[64,3584]{1,0:T(8,128)(2,1)S(1)}, u32[]{:S(2)}, u32[]{:S(2)}) %collective-permute-start.12) | collective-permute-done | bytes 458784 | tf_op jit(solution)/shard_map/ppermute | solution.py:22
  307.1 3.2 fusion.44
  312.8 7.8 %collective-permute-done.13 = bf16[64,3584]{1,0:T(8,128)(2,1)S(1)} collective-permute-done((bf16[64,3584]{1,0:T(8,128)(2,1)S(1)}, bf16[64,3584]{1,0:T(8,128)(2,1)S(1)}, u32[]{:S(2)}, u32[]{:S(2)}) %collective-permute-start.13) | collective-permute-done | bytes 458784 | tf_op jit(solution)/shard_map/ppermute | solution.py:22
  322.9 2.8 collective-permute-start.22
  326.1 7.0 %collective-permute-done.21 = bf16[64,3584]{1,0:T(8,128)(2,1)S(1)} collective-permute-done((bf16[64,3584]{1,0:T(8,128)(2,1)S(1)}, bf16[64,3584]{1,0:T(8,128)(2,1)S(1)}, u32[]{:S(2)}, u32[]{:S(2)}) %collective-permute-start.21) | collective-permute-done | bytes 458784 | tf_op jit(solution)/shard_map/ppermute | solution.py:22
  333.0 2.7 collective-permute-start.23
  335.9 8.9 %collective-permute-done.23 = bf16[64,3584]{1,0:T(8,128)(2,1)S(1)} collective-permute-done((bf16[64,3584]{1,0:T(8,128)(2,1)S(1)}, bf16[64,3584]{1,0:T(8,128)(2,1)S(1)}, u32[]{:S(2)}, u32[]{:S(2)}) %collective-permute-start.23) | collective-permute-done | bytes 458784 | tf_op jit(solution)/shard_map/ppermute | solution.py:22
  344.8 3.1 collective-permute-start.26
  348.0 5.1 %collective-permute-done.25 = bf16[64,3584]{1,0:T(8,128)(2,1)S(1)} collective-permute-done((bf16[64,3584]{1,0:T(8,128)(2,1)S(1)}, bf16[64,3584]{1,0:T(8,128)(2,1)S(1)}, u32[]{:S(2)}, u32[]{:S(2)}) %collective-permute-start.25) | collective-permute-done | bytes 458784 | tf_op jit(solution)/shard_map/ppermute | solution.py:22
  353.2 3.3 collective-permute-done.26
  361.2 2.8 collective-permute-start.51
  371.4 2.7 collective-permute-start.52
  374.9 10.6 %collective-permute-done.52 = bf16[64,3584]{1,0:T(8,128)(2,1)S(1)} collective-permute-done((bf16[64,3584]{1,0:T(8,128)(2,1)S(1)}, bf16[64,3584]{1,0:T(8,128)(2,1)S(1)}, u32[]{:S(2)}, u32[]{:S(2)}) %collective-permute-start.52) | collective-permute-done | bytes 458784 | tf_op jit(solution)/shard_map/ppermute | solution.py:22
  386.5 13.1 %collective-permute-done.54 = bf16[64,3584]{1,0:T(8,128)(2,1)S(1)} collective-permute-done((bf16[64,3584]{1,0:T(8,128)(2,1)S(1)}, bf16[64,3584]{1,0:T(8,128)(2,1)S(1)}, u32[]{:S(2)}, u32[]{:S(2)}) %collective-permute-start.54) | collective-permute-done | bytes 458784 | tf_op jit(solution)/shard_map/ppermute | solution.py:22
  401.1 7.7 %collective-permute-done.55 = bf16[64,3584]{1,0:T(8,128)(2,1)S(1)} collective-permute-done((bf16[64,3584]{1,0:T(8,128)(2,1)S(1)}, bf16[64,3584]{1,0:T(8,128)(2,1)S(1)}, u32[]{:S(2)}, u32[]{:S(2)}) %collective-permute-start.55) | collective-permute-done | bytes 458784 | tf_op jit(solution)/shard_map/ppermute | solution.py:22
  410.1 7.7 %collective-permute-done.56 = bf16[64,3584]{1,0:T(8,128)(2,1)S(1)} collective-permute-done((bf16[64,3584]{1,0:T(8,128)(2,1)S(1)}, bf16[64,3584]{1,0:T(8,128)(2,1)S(1)}, u32[]{:S(2)}, u32[]{:S(2)}) %collective-permute-start.56) | collective-permute-done | bytes 458784 | tf_op jit(solution)/shard_map/ppermute | solution.py:22
  424.6 2.7 collective-permute-start.61
  428.3 4.8 collective-permute-done.57
  437.4 6.4 %collective-permute-done.33 = bf16[64,3584]{1,0:T(8,128)(2,1)S(1)} collective-permute-done((bf16[64,3584]{1,0:T(8,128)(2,1)S(1)}, bf16[64,3584]{1,0:T(8,128)(2,1)S(1)}, u32[]{:S(2)}, u32[]{:S(2)}) %collective-permute-start.33) | collective-permute-done | bytes 458784 | tf_op jit(solution)/shard_map/ppermute | solution.py:22
  453.3 6.7 %fusion.41 = bf16[1,3584,1,384]{3,1,2,0:T(8,128)(2,1)} fusion(bf16[512,3584]{1,0:T(8,128)(2,1)S(1)} %copy-done.8, bf16[512,3584]{1,0:T(8,128)(2,1)S(1)} %copy-done.7, bf16[512,128]{0,1:T(8,128)(2,1)} %copy-done.33, bf16[512,128]{0,1:T(8,128)(2,1)} %copy-done.27, bf16[512,128]{0,1:T(8,128)(2,1)} %copy-done.28, bf16[512,128]{0,1:T(8,128)(2,1)} %copy-done.32, ...), kind=kOutput, calls=%fused_computation.47 | convolution fusion | flops 2839347200 | bytes 10878976 | tf_op jit(solution)/shard_map/na,nb->ab/dot_general | solution.py:65
  460.0 3.4 collective-permute-done.58
  466.0 3.1 fusion.106
  469.1 12.4 %collective-permute-start.35 = (bf16[64,3584]{1,0:T(8,128)(2,1)S(1)}, bf16[64,3584]{1,0:T(8,128)(2,1)S(1)}, u32[]{:S(2)}, u32[]{:S(2)}) collective-permute-start(bf16[64,3584]{1,0:T(8,128)(2,1)S(1)} %get-tuple-element.55), channel_id=1, source_target_pairs={{0,120},{8,0},{16,8},{24,16},{32,24},{40,32},{48,40},{56,48},{64,5... | collective-permute-start | bytes 1376264 | tf_op jit(solution)/shard_map/ppermute | solution.py:152
  486.0 8.9 %collective-permute-done.35 = bf16[64,3584]{1,0:T(8,128)(2,1)S(1)} collective-permute-done((bf16[64,3584]{1,0:T(8,128)(2,1)S(1)}, bf16[64,3584]{1,0:T(8,128)(2,1)S(1)}, u32[]{:S(2)}, u32[]{:S(2)}) %collective-permute-start.35) | collective-permute-done | bytes 458784 | tf_op jit(solution)/shard_map/ppermute | solution.py:152
  (278 shorter events, 120.2 us)
Async XLA Ops:
  0.7 66.5 %collective-permute-start.17 = (bf16[2,64,3584]{2,1,0:T(8,128)(2,1)}, bf16[2,64,3584]{2,1,0:T(8,128)(2,1)}, u32[]{:S(2)}, u32[]{:S(2)}) collective-permute-start(bf16[2,64,3584]{2,1,0:T(8,128)(2,1)} %bitcast.172), channel_id=1, source_target_pairs={{0,2},{1,3},{2,4},{3,5},{4,6},{5,7},{6,0},{7,1},{8,10},{9,11},{10,... | collective-permute-start | bytes 2752520 | tf_op jit(solution)/shard_map/ppermute | solution.py:22
  3.2 25.6 %collective-permute-start.15 = (bf16[2,64,3584]{2,1,0:T(8,128)(2,1)}, bf16[2,64,3584]{2,1,0:T(8,128)(2,1)}, u32[]{:S(2)}, u32[]{:S(2)}) collective-permute-start(bf16[2,64,3584]{2,1,0:T(8,128)(2,1)} %bitcast.173), channel_id=1, source_target_pairs={{0,6},{1,7},{2,0},{3,1},{4,2},{5,3},{6,4},{7,5},{8,14},{9,15},{10,... | collective-permute-start | bytes 2752520 | tf_op jit(solution)/shard_map/ppermute | solution.py:22
  5.4 21.2 %collective-permute-start.14 = (bf16[2,64,3584]{2,1,0:T(8,128)(2,1)}, bf16[2,64,3584]{2,1,0:T(8,128)(2,1)}, u32[]{:S(2)}, u32[]{:S(2)}) collective-permute-start(bf16[2,64,3584]{2,1,0:T(8,128)(2,1)} %bitcast.174), channel_id=1, source_target_pairs={{0,1},{1,0},{2,3},{3,2},{4,5},{5,4},{6,7},{7,6},{8,9},{9,8},{10,11... | collective-permute-start | bytes 2752520 | tf_op jit(solution)/shard_map/ppermute | solution.py:22
  10.4 39.4 %collective-permute-start.37 = (bf16[2,64,3584]{2,1,0:T(8,128)(2,1)}, bf16[2,64,3584]{2,1,0:T(8,128)(2,1)}, u32[]{:S(2)}, u32[]{:S(2)}) collective-permute-start(bf16[2,64,3584]{2,1,0:T(8,128)(2,1)} %get-tuple-element.57), channel_id=1, source_target_pairs={{0,6},{1,7},{2,0},{3,1},{4,2},{5,3},{6,4},{7,5},{8,14},{9,15},{10,... | collective-permute-start | bytes 2752520 | tf_op jit(solution)/shard_map/ppermute | solution.py:22
  11.8 34.5 %collective-permute-start.36 = (bf16[2,64,3584]{2,1,0:T(8,128)(2,1)}, bf16[2,64,3584]{2,1,0:T(8,128)(2,1)}, u32[]{:S(2)}, u32[]{:S(2)}) collective-permute-start(bf16[2,64,3584]{2,1,0:T(8,128)(2,1)} %get-tuple-element.57), channel_id=1, source_target_pairs={{0,1},{1,0},{2,3},{3,2},{4,5},{5,4},{6,7},{7,6},{8,9},{9,8},{10,11... | collective-permute-start | bytes 2752520 | tf_op jit(solution)/shard_map/ppermute | solution.py:22
  26.6 60.7 %collective-permute-start.39 = (bf16[2,64,3584]{2,1,0:T(8,128)(2,1)}, bf16[2,64,3584]{2,1,0:T(8,128)(2,1)S(1)}, u32[]{:S(2)}, u32[]{:S(2)}) collective-permute-start(bf16[2,64,3584]{2,1,0:T(8,128)(2,1)} %get-tuple-element.57), channel_id=1, source_target_pairs={{0,2},{1,3},{2,4},{3,5},{4,6},{5,7},{6,0},{7,1},{8,10},{9,11},{10,... | collective-permute-start | bytes 2752520 | tf_op jit(solution)/shard_map/ppermute | solution.py:22
  28.8 39.0 %collective-permute-start.1 = (bf16[2,64,3584]{2,1,0:T(8,128)(2,1)S(1)}, bf16[2,64,3584]{2,1,0:T(8,128)(2,1)S(1)}, u32[]{:S(2)}, u32[]{:S(2)}) collective-permute-start(bf16[2,64,3584]{2,1,0:T(8,128)(2,1)S(1)} %get-tuple-element.63), channel_id=1, source_target_pairs={{0,6},{1,7},{2,0},{3,1},{4,2},{5,3},{6,4},{7,5},{8,14},{9,15},{10,... | collective-permute-start | bytes 2752520 | tf_op jit(solution)/shard_map/ppermute | solution.py:22
  46.3 20.0 %collective-permute-start = (bf16[2,64,3584]{2,1,0:T(8,128)(2,1)S(1)}, bf16[2,64,3584]{2,1,0:T(8,128)(2,1)S(1)}, u32[]{:S(2)}, u32[]{:S(2)}) collective-permute-start(bf16[2,64,3584]{2,1,0:T(8,128)(2,1)S(1)} %get-tuple-element.63), channel_id=1, source_target_pairs={{0,1},{1,0},{2,3},{3,2},{4,5},{5,4},{6,7},{7,6},{8,9},{9,8},{10,11... | collective-permute-start | bytes 2752520 | tf_op jit(solution)/shard_map/ppermute | solution.py:22
  49.8 64.8 %collective-permute-start.3 = (bf16[2,64,3584]{2,1,0:T(8,128)(2,1)S(1)}, bf16[2,64,3584]{2,1,0:T(8,128)(2,1)S(1)}, u32[]{:S(2)}, u32[]{:S(2)}) collective-permute-start(bf16[2,64,3584]{2,1,0:T(8,128)(2,1)S(1)} %get-tuple-element.63), channel_id=1, source_target_pairs={{0,2},{1,3},{2,4},{3,5},{4,6},{5,7},{6,0},{7,1},{8,10},{9,11},{10,... | collective-permute-start | bytes 2752520 | tf_op jit(solution)/shard_map/ppermute | solution.py:22
  66.3 19.3 %collective-permute-start.16 = (bf16[2,64,3584]{2,1,0:T(8,128)(2,1)}, bf16[2,64,3584]{2,1,0:T(8,128)(2,1)S(1)}, u32[]{:S(2)}, u32[]{:S(2)}) collective-permute-start(bf16[2,64,3584]{2,1,0:T(8,128)(2,1)} %collective-permute-done.14), channel_id=1, source_target_pairs={{0,6},{1,7},{2,0},{3,1},{4,2},{5,3},{6,4},{7,5},{8,14},{9,15},{10,... | collective-permute-start | bytes 2752520 | tf_op jit(solution)/shard_map/ppermute | solution.py:22
  67.1 124.1 %collective-permute-start.20 = (bf16[2,64,3584]{2,1,0:T(8,128)(2,1)}, bf16[2,64,3584]{2,1,0:T(8,128)(2,1)S(1)}, u32[]{:S(2)}, u32[]{:S(2)}) collective-permute-start(bf16[2,64,3584]{2,1,0:T(8,128)(2,1)} %collective-permute-done.14), channel_id=1, source_target_pairs={{0,2},{1,3},{2,4},{3,5},{4,6},{5,7},{6,0},{7,1},{8,10},{9,11},{10,... | collective-permute-start | bytes 2752520 | tf_op jit(solution)/shard_map/ppermute | solution.py:22
  67.9 42.8 %collective-permute-start.18 = (bf16[2,64,3584]{2,1,0:T(8,128)(2,1)}, bf16[2,64,3584]{2,1,0:T(8,128)(2,1)S(1)}, u32[]{:S(2)}, u32[]{:S(2)}) collective-permute-start(bf16[2,64,3584]{2,1,0:T(8,128)(2,1)} %collective-permute-done.17), channel_id=1, source_target_pairs={{0,2},{1,3},{2,4},{3,5},{4,6},{5,7},{6,0},{7,1},{8,10},{9,11},{10,... | collective-permute-start | bytes 2752520 | tf_op jit(solution)/shard_map/ppermute | solution.py:22
  85.5 25.3 %collective-permute-start.38 = (bf16[2,64,3584]{2,1,0:T(8,128)(2,1)}, bf16[2,64,3584]{2,1,0:T(8,128)(2,1)S(1)}, u32[]{:S(2)}, u32[]{:S(2)}) collective-permute-start(bf16[2,64,3584]{2,1,0:T(8,128)(2,1)} %collective-permute-done.36), channel_id=1, source_target_pairs={{0,6},{1,7},{2,0},{3,1},{4,2},{5,3},{6,4},{7,5},{8,14},{9,15},{10,... | collective-permute-start | bytes 2752520 | tf_op jit(solution)/shard_map/ppermute | solution.py:22
  87.3 126.9 %collective-permute-start.42 = (bf16[2,64,3584]{2,1,0:T(8,128)(2,1)}, bf16[2,64,3584]{2,1,0:T(8,128)(2,1)S(1)}, u32[]{:S(2)}, u32[]{:S(2)}) collective-permute-start(bf16[2,64,3584]{2,1,0:T(8,128)(2,1)} %collective-permute-done.36), channel_id=1, source_target_pairs={{0,2},{1,3},{2,4},{3,5},{4,6},{5,7},{6,0},{7,1},{8,10},{9,11},{10,... | collective-permute-start | bytes 2752520 | tf_op jit(solution)/shard_map/ppermute | solution.py:22
  110.7 39.3 %collective-permute-start.40 = (bf16[2,64,3584]{2,1,0:T(8,128)(2,1)S(1)}, bf16[2,64,3584]{2,1,0:T(8,128)(2,1)S(1)}, u32[]{:S(2)}, u32[]{:S(2)}) collective-permute-start(bf16[2,64,3584]{2,1,0:T(8,128)(2,1)S(1)} %collective-permute-done.39), channel_id=1, source_target_pairs={{0,2},{1,3},{2,4},{3,5},{4,6},{5,7},{6,0},{7,1},{8,10},{9,11},{10,... | collective-permute-start | bytes 2752520 | tf_op jit(solution)/shard_map/ppermute | solution.py:22
  110.8 40.3 %collective-permute-start.2 = (bf16[2,64,3584]{2,1,0:T(8,128)(2,1)S(1)}, bf16[2,64,3584]{2,1,0:T(8,128)(2,1)S(1)}, u32[]{:S(2)}, u32[]{:S(2)}) collective-permute-start(bf16[2,64,3584]{2,1,0:T(8,128)(2,1)S(1)} %collective-permute-done), channel_id=1, source_target_pairs={{0,6},{1,7},{2,0},{3,1},{4,2},{5,3},{6,4},{7,5},{8,14},{9,15},{10,... | collective-permute-start | bytes 2752520 | tf_op jit(solution)/shard_map/ppermute | solution.py:22
  114.5 114.3 %collective-permute-start.6 = (bf16[2,64,3584]{2,1,0:T(8,128)(2,1)S(1)}, bf16[2,64,3584]{2,1,0:T(8,128)(2,1)S(1)}, u32[]{:S(2)}, u32[]{:S(2)}) collective-permute-start(bf16[2,64,3584]{2,1,0:T(8,128)(2,1)S(1)} %collective-permute-done), channel_id=1, source_target_pairs={{0,2},{1,3},{2,4},{3,5},{4,6},{5,7},{6,0},{7,1},{8,10},{9,11},{10,... | collective-permute-start | bytes 2752520 | tf_op jit(solution)/shard_map/ppermute | solution.py:22
  150.0 39.3 %collective-permute-start.4 = (bf16[2,64,3584]{2,1,0:T(8,128)(2,1)S(1)}, bf16[2,64,3584]{2,1,0:T(8,128)(2,1)S(1)}, u32[]{:S(2)}, u32[]{:S(2)}) collective-permute-start(bf16[2,64,3584]{2,1,0:T(8,128)(2,1)S(1)} %collective-permute-done.3), channel_id=1, source_target_pairs={{0,2},{1,3},{2,4},{3,5},{4,6},{5,7},{6,0},{7,1},{8,10},{9,11},{10,... | collective-permute-start | bytes 2752520 | tf_op jit(solution)/shard_map/ppermute | solution.py:22
  151.0 38.4 %collective-permute-start.19 = (bf16[2,64,3584]{2,1,0:T(8,128)(2,1)S(1)}, bf16[2,64,3584]{2,1,0:T(8,128)(2,1)S(1)}, u32[]{:S(2)}, u32[]{:S(2)}) collective-permute-start(bf16[2,64,3584]{2,1,0:T(8,128)(2,1)S(1)} %collective-permute-done.16), channel_id=1, source_target_pairs={{0,6},{1,7},{2,0},{3,1},{4,2},{5,3},{6,4},{7,5},{8,14},{9,15},{10,... | collective-permute-start | bytes 2752520 | tf_op jit(solution)/shard_map/ppermute | solution.py:22
  189.4 19.5 %collective-permute-start.41 = (bf16[2,64,3584]{2,1,0:T(8,128)(2,1)S(1)}, bf16[2,64,3584]{2,1,0:T(8,128)(2,1)S(1)}, u32[]{:S(2)}, u32[]{:S(2)}) collective-permute-start(bf16[2,64,3584]{2,1,0:T(8,128)(2,1)S(1)} %collective-permute-done.38), channel_id=1, source_target_pairs={{0,6},{1,7},{2,0},{3,1},{4,2},{5,3},{6,4},{7,5},{8,14},{9,15},{10,... | collective-permute-start | bytes 2752520 | tf_op jit(solution)/shard_map/ppermute | solution.py:22
  189.4 39.1 %collective-permute-start.5 = (bf16[2,64,3584]{2,1,0:T(8,128)(2,1)S(1)}, bf16[2,64,3584]{2,1,0:T(8,128)(2,1)S(1)}, u32[]{:S(2)}, u32[]{:S(2)}) collective-permute-start(bf16[2,64,3584]{2,1,0:T(8,128)(2,1)S(1)} %collective-permute-done.2), channel_id=1, source_target_pairs={{0,6},{1,7},{2,0},{3,1},{4,2},{5,3},{6,4},{7,5},{8,14},{9,15},{10,... | collective-permute-start | bytes 2752520 | tf_op jit(solution)/shard_map/ppermute | solution.py:22
  241.3 26.3 %collective-permute-start.43 = (bf16[64,3584]{1,0:T(8,128)(2,1)}, bf16[64,3584]{1,0:T(8,128)(2,1)}, u32[]{:S(2)}, u32[]{:S(2)}) collective-permute-start(bf16[64,3584]{1,0:T(8,128)(2,1)} %get-tuple-element.39), channel_id=1, source_target_pairs={{0,2},{1,3},{2,4},{3,5},{4,6},{5,7},{6,0},{7,1},{8,10},{9,11},{10,... | collective-permute-start | bytes 1376264 | tf_op jit(solution)/shard_map/ppermute | solution.py:22
  241.3 29.0 %collective-permute-start.47 = (bf16[64,3584]{1,0:T(8,128)(2,1)}, bf16[64,3584]{1,0:T(8,128)(2,1)}, u32[]{:S(2)}, u32[]{:S(2)}) collective-permute-start(bf16[64,3584]{1,0:T(8,128)(2,1)} %get-tuple-element.40), channel_id=1, source_target_pairs={{0,6},{1,7},{2,0},{3,1},{4,2},{5,3},{6,4},{7,5},{8,14},{9,15},{10,... | collective-permute-start | bytes 1376264 | tf_op jit(solution)/shard_map/ppermute | solution.py:22
  243.9 36.1 %collective-permute-start.46 = (bf16[64,3584]{1,0:T(8,128)(2,1)}, bf16[64,3584]{1,0:T(8,128)(2,1)S(1)}, u32[]{:S(2)}, u32[]{:S(2)}) collective-permute-start(bf16[64,3584]{1,0:T(8,128)(2,1)} %get-tuple-element.41), channel_id=1, source_target_pairs={{0,2},{1,3},{2,4},{3,5},{4,6},{5,7},{6,0},{7,1},{8,10},{9,11},{10,... | collective-permute-start | bytes 1376264 | tf_op jit(solution)/shard_map/ppermute | solution.py:22
  243.9 61.4 %collective-permute-start.45 = (bf16[64,3584]{1,0:T(8,128)(2,1)S(1)}, bf16[64,3584]{1,0:T(8,128)(2,1)S(1)}, u32[]{:S(2)}, u32[]{:S(2)}) collective-permute-start(bf16[64,3584]{1,0:T(8,128)(2,1)S(1)} %get-tuple-element.42), channel_id=1, source_target_pairs={{0,6},{1,7},{2,0},{3,1},{4,2},{5,3},{6,4},{7,5},{8,14},{9,15},{10,... | collective-permute-start | bytes 1376264 | tf_op jit(solution)/shard_map/ppermute | solution.py:22
  252.8 18.8 %collective-permute-start.7 = (bf16[64,3584]{1,0:T(8,128)(2,1)}, bf16[64,3584]{1,0:T(8,128)(2,1)}, u32[]{:S(2)}, u32[]{:S(2)}) collective-permute-start(bf16[64,3584]{1,0:T(8,128)(2,1)} %get-tuple-element.45), channel_id=1, source_target_pairs={{0,2},{1,3},{2,4},{3,5},{4,6},{5,7},{6,0},{7,1},{8,10},{9,11},{10,... | collective-permute-start | bytes 1376264 | tf_op jit(solution)/shard_map/ppermute | solution.py:22
  270.2 28.4 %collective-permute-start.10 = (bf16[64,3584]{1,0:T(8,128)(2,1)S(1)}, bf16[64,3584]{1,0:T(8,128)(2,1)S(1)}, u32[]{:S(2)}, u32[]{:S(2)}) collective-permute-start(bf16[64,3584]{1,0:T(8,128)(2,1)S(1)} %copy-done.13), channel_id=1, source_target_pairs={{0,2},{1,3},{2,4},{3,5},{4,6},{5,7},{6,0},{7,1},{8,10},{9,11},{10,... | collective-permute-start | bytes 1376264 | tf_op jit(solution)/shard_map/ppermute | solution.py:22
  271.6 38.7 %collective-permute-start.9 = (bf16[64,3584]{1,0:T(8,128)(2,1)S(1)}, bf16[64,3584]{1,0:T(8,128)(2,1)S(1)}, u32[]{:S(2)}, u32[]{:S(2)}) collective-permute-start(bf16[64,3584]{1,0:T(8,128)(2,1)S(1)} %get-tuple-element.48), channel_id=1, source_target_pairs={{0,6},{1,7},{2,0},{3,1},{4,2},{5,3},{6,4},{7,5},{8,14},{9,15},{10,... | collective-permute-start | bytes 1376264 | tf_op jit(solution)/shard_map/ppermute | solution.py:22
  275.7 19.4 %collective-permute-start.48 = (bf16[64,3584]{1,0:T(8,128)(2,1)S(1)}, bf16[64,3584]{1,0:T(8,128)(2,1)S(1)}, u32[]{:S(2)}, u32[]{:S(2)}) collective-permute-start(bf16[64,3584]{1,0:T(8,128)(2,1)S(1)} %get-tuple-element.38), channel_id=1, source_target_pairs={{0,6},{1,7},{2,0},{3,1},{4,2},{5,3},{6,4},{7,5},{8,14},{9,15},{10,... | collective-permute-start | bytes 1376264 | tf_op jit(solution)/shard_map/ppermute | solution.py:22
  280.0 30.3 %collective-permute-start.44 = (bf16[64,3584]{1,0:T(8,128)(2,1)S(1)}, bf16[64,3584]{1,0:T(8,128)(2,1)S(1)}, u32[]{:S(2)}, u32[]{:S(2)}) collective-permute-start(bf16[64,3584]{1,0:T(8,128)(2,1)S(1)} %get-tuple-element.37), channel_id=1, source_target_pairs={{0,2},{1,3},{2,4},{3,5},{4,6},{5,7},{6,0},{7,1},{8,10},{9,11},{10,... | collective-permute-start | bytes 1376264 | tf_op jit(solution)/shard_map/ppermute | solution.py:22
  305.3 15.3 %collective-permute-start.13 = (bf16[64,3584]{1,0:T(8,128)(2,1)S(1)}, bf16[64,3584]{1,0:T(8,128)(2,1)S(1)}, u32[]{:S(2)}, u32[]{:S(2)}) collective-permute-start(bf16[64,3584]{1,0:T(8,128)(2,1)S(1)} %add_convert_fusion.9), channel_id=1, source_target_pairs={{0,1},{1,0},{2,3},{3,2},{4,5},{5,4},{6,7},{7,6},{8,9},{9,8},{10,11... | collective-permute-start | bytes 1376264 | tf_op jit(solution)/shard_map/ppermute | solution.py:22
  322.9 12.8 %collective-permute-start.24 = (bf16[64,3584]{1,0:T(8,128)(2,1)S(1)}, bf16[64,3584]{1,0:T(8,128)(2,1)S(1)}, u32[]{:S(2)}, u32[]{:S(2)}) collective-permute-start(bf16[64,3584]{1,0:T(8,128)(2,1)S(1)} %get-tuple-element.21), channel_id=1, source_target_pairs={{0,2},{1,3},{2,4},{3,5},{4,6},{5,7},{6,0},{7,1},{8,10},{9,11},{10,... | collective-permute-start | bytes 1376264 | tf_op jit(solution)/shard_map/ppermute | solution.py:22
  322.9 12.9 %collective-permute-start.22 = (bf16[64,3584]{1,0:T(8,128)(2,1)S(1)}, bf16[64,3584]{1,0:T(8,128)(2,1)S(1)}, u32[]{:S(2)}, u32[]{:S(2)}) collective-permute-start(bf16[64,3584]{1,0:T(8,128)(2,1)S(1)} %get-tuple-element.21), channel_id=1, source_target_pairs={{0,6},{1,7},{2,0},{3,1},{4,2},{5,3},{6,4},{7,5},{8,14},{9,15},{10,... | collective-permute-start | bytes 1376264 | tf_op jit(solution)/shard_map/ppermute | solution.py:22
  333.0 23.6 %collective-permute-start.27 = (bf16[64,3584]{1,0:T(8,128)(2,1)S(1)}, bf16[64,3584]{1,0:T(8,128)(2,1)S(1)}, u32[]{:S(2)}, u32[]{:S(2)}) collective-permute-start(bf16[64,3584]{1,0:T(8,128)(2,1)S(1)} %collective-permute-done.21), channel_id=1, source_target_pairs={{0,2},{1,3},{2,4},{3,5},{4,6},{5,7},{6,0},{7,1},{8,10},{9,11},{10,... | collective-permute-start | bytes 1376264 | tf_op jit(solution)/shard_map/ppermute | solution.py:22
  335.7 17.4 %collective-permute-start.25 = (bf16[64,3584]{1,0:T(8,128)(2,1)S(1)}, bf16[64,3584]{1,0:T(8,128)(2,1)S(1)}, u32[]{:S(2)}, u32[]{:S(2)}) collective-permute-start(bf16[64,3584]{1,0:T(8,128)(2,1)S(1)} %collective-permute-done.24), channel_id=1, source_target_pairs={{0,2},{1,3},{2,4},{3,5},{4,6},{5,7},{6,0},{7,1},{8,10},{9,11},{10,... | collective-permute-start | bytes 1376264 | tf_op jit(solution)/shard_map/ppermute | solution.py:22
  360.8 13.3 %collective-permute-start.53 = (bf16[64,3584]{1,0:T(8,128)(2,1)S(1)}, bf16[64,3584]{1,0:T(8,128)(2,1)S(1)}, u32[]{:S(2)}, u32[]{:S(2)}) collective-permute-start(bf16[64,3584]{1,0:T(8,128)(2,1)S(1)} %get-tuple-element.18), channel_id=1, source_target_pairs={{0,2},{1,3},{2,4},{3,5},{4,6},{5,7},{6,0},{7,1},{8,10},{9,11},{10,... | collective-permute-start | bytes 1376264 | tf_op jit(solution)/shard_map/ppermute | solution.py:22
  366.2 58.4 %collective-permute-start.28 = (bf16[64,3584]{1,0:T(8,128)(2,1)S(1)}, bf16[64,3584]{1,0:T(8,128)(2,1)S(1)}, u32[]{:S(2)}, u32[]{:S(2)}) collective-permute-start(bf16[64,3584]{1,0:T(8,128)(2,1)S(1)} %get-tuple-element.33), channel_id=1, source_target_pairs={{0,2},{1,3},{2,4},{3,5},{4,6},{5,7},{6,0},{7,1},{8,10},{9,11},{10,... | collective-permute-start | bytes 1376264 | tf_op jit(solution)/shard_map/ppermute | solution.py:22
  366.3 60.9 %collective-permute-start.32 = (bf16[64,3584]{1,0:T(8,128)(2,1)S(1)}, bf16[64,3584]{1,0:T(8,128)(2,1)S(1)}, u32[]{:S(2)}, u32[]{:S(2)}) collective-permute-start(bf16[64,3584]{1,0:T(8,128)(2,1)S(1)} %get-tuple-element.34), channel_id=1, source_target_pairs={{0,6},{1,7},{2,0},{3,1},{4,2},{5,3},{6,4},{7,5},{8,14},{9,15},{10,... | collective-permute-start | bytes 1376264 | tf_op jit(solution)/shard_map/ppermute | solution.py:22
  371.3 64.3 %collective-permute-start.31 = (bf16[64,3584]{1,0:T(8,128)(2,1)S(1)}, bf16[64,3584]{1,0:T(8,128)(2,1)S(1)}, u32[]{:S(2)}, u32[]{:S(2)}) collective-permute-start(bf16[64,3584]{1,0:T(8,128)(2,1)S(1)} %get-tuple-element.35), channel_id=1, source_target_pairs={{0,2},{1,3},{2,4},{3,5},{4,6},{5,7},{6,0},{7,1},{8,10},{9,11},{10,... | collective-permute-start | bytes 1376264 | tf_op jit(solution)/shard_map/ppermute | solution.py:22
  371.4 14.2 %collective-permute-start.52 = (bf16[64,3584]{1,0:T(8,128)(2,1)S(1)}, bf16[64,3584]{1,0:T(8,128)(2,1)S(1)}, u32[]{:S(2)}, u32[]{:S(2)}) collective-permute-start(bf16[64,3584]{1,0:T(8,128)(2,1)S(1)} %collective-permute-done.50), channel_id=1, source_target_pairs={{0,6},{1,7},{2,0},{3,1},{4,2},{5,3},{6,4},{7,5},{8,14},{9,15},{10,... | collective-permute-start | bytes 1376264 | tf_op jit(solution)/shard_map/ppermute | solution.py:22
  374.2 77.5 %collective-permute-start.30 = (bf16[64,3584]{1,0:T(8,128)(2,1)S(1)}, bf16[64,3584]{1,0:T(8,128)(2,1)S(1)}, u32[]{:S(2)}, u32[]{:S(2)}) collective-permute-start(bf16[64,3584]{1,0:T(8,128)(2,1)S(1)} %get-tuple-element.36), channel_id=1, source_target_pairs={{0,6},{1,7},{2,0},{3,1},{4,2},{5,3},{6,4},{7,5},{8,14},{9,15},{10,... | collective-permute-start | bytes 1376264 | tf_op jit(solution)/shard_map/ppermute | solution.py:22
  385.5 14.1 %collective-permute-start.54 = (bf16[64,3584]{1,0:T(8,128)(2,1)S(1)}, bf16[64,3584]{1,0:T(8,128)(2,1)S(1)}, u32[]{:S(2)}, u32[]{:S(2)}) collective-permute-start(bf16[64,3584]{1,0:T(8,128)(2,1)S(1)} %collective-permute-done.53), channel_id=1, source_target_pairs={{0,2},{1,3},{2,4},{3,5},{4,6},{5,7},{6,0},{7,1},{8,10},{9,11},{10,... | collective-permute-start | bytes 1376264 | tf_op jit(solution)/shard_map/ppermute | solution.py:22
  428.3 31.7 %collective-permute-start.29 = (bf16[64,3584]{1,0:T(8,128)(2,1)}, bf16[64,3584]{1,0:T(8,128)(2,1)}, u32[]{:S(2)}, u32[]{:S(2)}) collective-permute-start(bf16[64,3584]{1,0:T(8,128)(2,1)} %get-tuple-element.31), channel_id=1, source_target_pairs={{0,2},{1,3},{2,4},{3,5},{4,6},{5,7},{6,0},{7,1},{8,10},{9,11},{10,... | collective-permute-start | bytes 1376264 | tf_op jit(solution)/shard_map/ppermute | solution.py:22
  433.7 13.9 %collective-permute-start.60 = (bf16[64,3584]{1,0:T(8,128)(2,1)S(1)}, bf16[64,3584]{1,0:T(8,128)(2,1)S(1)}, u32[]{:S(2)}, u32[]{:S(2)}) collective-permute-start(bf16[64,3584]{1,0:T(8,128)(2,1)S(1)} %get-tuple-element.29), channel_id=1, source_target_pairs={{0,2},{1,3},{2,4},{3,5},{4,6},{5,7},{6,0},{7,1},{8,10},{9,11},{10,... | collective-permute-start | bytes 1376264 | tf_op jit(solution)/shard_map/ppermute | solution.py:22
  435.6 15.1 %collective-permute-start.62 = (bf16[64,3584]{1,0:T(8,128)(2,1)S(1)}, bf16[64,3584]{1,0:T(8,128)(2,1)S(1)}, u32[]{:S(2)}, u32[]{:S(2)}) collective-permute-start(bf16[64,3584]{1,0:T(8,128)(2,1)S(1)} %get-tuple-element.26), channel_id=1, source_target_pairs={{0,6},{1,7},{2,0},{3,1},{4,2},{5,3},{6,4},{7,5},{8,14},{9,15},{10,... | collective-permute-start | bytes 1376264 | tf_op jit(solution)/shard_map/ppermute | solution.py:22
  444.8 15.2 %collective-permute-start.34 = (bf16[64,3584]{1,0:T(8,128)(2,1)}, bf16[64,3584]{1,0:T(8,128)(2,1)}, u32[]{:S(2)}, u32[]{:S(2)}) collective-permute-start(bf16[64,3584]{1,0:T(8,128)(2,1)} %add_convert_fusion.6), channel_id=1, source_target_pairs={{0,1},{1,0},{2,3},{3,2},{4,5},{5,4},{6,7},{7,6},{8,9},{9,8},{10,11... | collective-permute-start | bytes 1376264 | tf_op jit(solution)/shard_map/ppermute | solution.py:22
  469.1 25.8 %collective-permute-start.35 = (bf16[64,3584]{1,0:T(8,128)(2,1)S(1)}, bf16[64,3584]{1,0:T(8,128)(2,1)S(1)}, u32[]{:S(2)}, u32[]{:S(2)}) collective-permute-start(bf16[64,3584]{1,0:T(8,128)(2,1)S(1)} %get-tuple-element.55), channel_id=1, source_target_pairs={{0,120},{8,0},{16,8},{24,16},{32,24},{40,32},{48,40},{56,48},{64,5... | collective-permute-start | bytes 1376264 | tf_op jit(solution)/shard_map/ppermute | solution.py:152
  481.5 13.4 %collective-permute-start.64 = (bf16[64,3584]{1,0:T(8,128)(2,1)S(1)}, bf16[64,3584]{1,0:T(8,128)(2,1)S(1)}, u32[]{:S(2)}, u32[]{:S(2)}) collective-permute-start(bf16[64,3584]{1,0:T(8,128)(2,1)S(1)} %get-tuple-element.56), channel_id=1, source_target_pairs={{0,8},{8,16},{16,24},{24,32},{32,40},{40,48},{48,56},{56,64},{64,7... | collective-permute-start | bytes 1376264 | tf_op jit(solution)/shard_map/ppermute | solution.py:152
  (56 other events, 939.8 us)
